TPU v7x, 32 devices: a whole 2x2x4 slice. The times are simulated.
32 devices in a mesh: groups: 2 (over x), seq: 16 (over z, y, core).
Axes of the slice: x: 2, y: 2, z: 4, core: 2. Of those that a mesh axis runs over, the one named last changes fastest.
Arguments:
- tokens: bfloat16 [32768, 2048], P(('groups', 'seq')), parts along dimension 0, may hold values from -64 to 64, as said below
- gain_mix: float32 [2048], replicated, may hold values from 0.1 to 1.9
- gain_mlp: float32 [2048], replicated, may hold values from 0.1 to 1.9
- block_mix: bfloat16 [1024, 1024], replicated, may hold values from -0.1875 to 0.1875
- cross_mix: bfloat16 [16, 16], replicated, may hold values from -1.5 to 1.5
- w_in: bfloat16 [2048, 1024], P('seq'), may hold values from -0.25 to 0.25
- w_out: bfloat16 [4096, 512], P('seq'), may hold values from -0.1875 to 0.1875
Outputs:
- mixed: bfloat16 [32768, 2048], P(('groups', 'seq')), parts along dimension 0
There are 2 independent parts, one for each index of `groups`. A program takes and returns all parts, laid end to end along the dimension named above; an argument that names none is the same for every part. Nothing has to cross between parts.
Inputs may be any that keep to these rules, and one draw needn't show every extreme that they name: `tokens`: activations with independent scales per channel and per position.
All inputs are finite; a program needn't handle non-finite values.
Results may differ from a plain program's by a relative error of at most 0.0085.
Values may be sent and summed in bfloat16 or wider, within the bound.
A program may use at most 128 MiB of HBM per device.

v0:
```python
import jax
import jax.numpy as jnp
from jax import lax
from jax.sharding import PartitionSpec as P

NCB = 4
BLK = 1024


def rms_scale(values, gain):
    mean_square = jnp.mean(values * values, axis=-1, keepdims=True)
    return values * lax.rsqrt(mean_square + 1e-06) * gain


def shards(tokens, gain_mix, gain_mlp, block_mix, cross_mix, w_in, w_out):
    rows, width = tokens.shape
    nblocks = rows // BLK
    raw = tokens.astype(jnp.float32)
    normed = rms_scale(raw, gain_mix).astype(jnp.bfloat16)
    within = jnp.einsum(
        "hp,ops->ohs",
        block_mix,
        normed.reshape(nblocks, BLK, width),
        preferred_element_type=jnp.float32,
    ).astype(jnp.bfloat16)
    mixed_cols = jnp.einsum(
        "ai,ijd->ajd",
        cross_mix,
        lax.all_to_all(within, "seq", split_axis=1, concat_axis=0, tiled=True),
        preferred_element_type=jnp.float32,
    ).astype(jnp.bfloat16)
    across = lax.all_to_all(mixed_cols, "seq", split_axis=0, concat_axis=1, tiled=True)
    gated = (
        raw + normed.astype(jnp.float32) * across.reshape(rows, width).astype(jnp.float32)
    ).astype(jnp.bfloat16)
    inner = rms_scale(gated.astype(jnp.float32), gain_mlp).astype(jnp.bfloat16)
    weight_in = lax.all_gather(w_in, "seq", axis=0, tiled=True)
    hidden = jnp.einsum(
        "rcd,cdf->rcf",
        inner.reshape(rows, NCB, width // NCB),
        weight_in.reshape(NCB, width // NCB, -1),
        preferred_element_type=jnp.float32,
    )
    hidden = jax.nn.gelu(hidden).astype(jnp.bfloat16)
    weight_out = lax.all_gather(w_out, "seq", axis=0, tiled=True)
    output = jnp.einsum(
        "rcf,cfd->rcd",
        hidden,
        weight_out.reshape(NCB, hidden.shape[2], -1),
        preferred_element_type=jnp.float32,
    )
    return (gated.astype(jnp.float32) + output.reshape(rows, width)).astype(jnp.bfloat16)


def solution(mesh):
    in_specs = (P(("groups", "seq"), None), P(), P(), P(), P(), P("seq", None), P("seq", None))
    out_specs = P(("groups", "seq"), None)
    return jax.shard_map(shards, mesh=mesh, in_specs=in_specs, out_specs=out_specs, check_vma=False)
```

profile of v0, /device:TPU:13, one launch (start us, length us, event | category | flops | bytes accessed | tf_op | source)
XLA Modules:
  0.0 401.5 jit_solution(3762509726161138529)
XLA Ops:
  6.5 3.2 fusion.8
  9.8 9.2 %convert_bitcast_fusion.1 = bf16[1,1024,2048]{1,2,0:T(8,128)(2,1)} fusion(bf16[1024,1024]{1,0:T(8,128)(2,1)S(1)} %copy-done, bf16[1024,2048]{1,0:T(8,128)(2,1)} %param.7, f32[2048]{0:T(1024)} %param.8, f32[1024]{0:T(1024)S(1)} %add_rsqrt_fusion.1), kind=kOutput, calls=%fused_computation.29 | convolution fusion | flops 4305453056 | bytes 10498048 | tf_op jit(solution)/shard_map/hp,ops->ohs/dot_general | solution.py:20
  19.0 20.6 %copy.17 = bf16[1,1024,2048]{2,0,1:T(2,128)(2,1)} copy(bf16[1,1024,2048]{1,2,0:T(8,128)(2,1)} %convert_bitcast_fusion.1) | data formatting | bytes 8388608 | tf_op jit(solution)/shard_map/convert_element_type | solution.py:25
  39.6 0.5 broadcast.36
  40.2 26.7 %reduce = bf16[1024,2048]{1,0:T(8,128)(2,1)} reduce(bf16[1024,1,2048]{2,1,0:T(2,128)(2,1)} %bitcast.34, bf16[]{:T(256)} %broadcast.36), dimensions={1}, to_apply=%bitcast.28.reduce_sub_computation | reduce | bytes 8388610
  66.9 11.4 %reshape.51 = bf16[16,2,65536]{2,1,0:T(2,128)(2,1)} reshape(bf16[1024,2048]{1,0:T(8,128)(2,1)} %reduce) | data formatting | bytes 8388608
  78.3 6.6 %all-to-all-start = ((bf16[16,2,65536]{2,1,0:T(2,128)(2,1)}), bf16[16,2,65536]{2,1,0:T(2,128)(2,1)}, u32[]{:S(2)}, u32[]{:S(2)}) async-start(bf16[16,2,65536]{2,1,0:T(2,128)(2,1)} %reshape.51), calls=%async_computation | async-start | bytes 8388608 | tf_op jit(solution)/shard_map/all_to_all | solution.py:29
  84.8 0.2 all-gather.3.cloned.1.call-start
  85.0 0.5 all-gather.3.cloned.1.call-update
  85.5 117.0 %all-to-all-done = bf16[16,2,65536]{2,1,0:T(2,128)(2,1)} async-done(((bf16[16,2,65536]{2,1,0:T(2,128)(2,1)}), bf16[16,2,65536]{2,1,0:T(2,128)(2,1)}, u32[]{:S(2)}, u32[]{:S(2)}) %all-to-all-start) | async-done | bytes 4194336 | tf_op jit(solution)/shard_map/all_to_all | solution.py:29
  202.6 12.4 %reshape.52 = bf16[1024,1,2048]{2,1,0:T(2,128)(2,1)} reshape(bf16[16,2,65536]{2,1,0:T(2,128)(2,1)} %all-to-all-done) | data formatting | bytes 8388608
  214.9 6.0 %copy.24 = bf16[1,1024,2048]{2,1,0:T(8,128)(2,1)S(1)} copy(bf16[1,1024,2048]{2,0,1:T(2,128)(2,1)} %bitcast.35) | data formatting | bytes 8388608
  221.0 4.8 %convert_bitcast_fusion = bf16[16,64,2048]{2,0,1:T(8,128)(2,1)S(1)} fusion(bf16[16,64,2048]{2,1,0:T(8,128)(2,1)S(1)} %bitcast.36, bf16[16,16]{1,0:T(8,128)(2,1)S(1)} %copy-done.5), kind=kOutput, calls=%fused_computation.28 | convolution fusion | flops 69206016 | bytes 8389120 | tf_op jit(solution)/shard_map/ai,ijd->ajd/dot_general | solution.py:26
  225.8 4.3 %copy.19 = bf16[16,64,2048]{2,1,0:T(8,128)(2,1)} copy(bf16[16,64,2048]{2,0,1:T(8,128)(2,1)S(1)} %convert_bitcast_fusion) | data formatting | bytes 8388608 | tf_op jit(solution)/shard_map/convert_element_type | solution.py:31
  230.1 4.9 %all-to-all-start.1 = ((bf16[16,64,2048]{2,1,0:T(8,128)(2,1)}), bf16[16,64,2048]{2,1,0:T(8,128)(2,1)}, u32[]{:S(2)}, u32[]{:S(2)}) async-start(bf16[16,64,2048]{2,1,0:T(8,128)(2,1)} %copy.19), calls=%async_computation.1 | async-start | bytes 8388608 | tf_op jit(solution)/shard_map/all_to_all | solution.py:32
  235.0 0.3 all-gather.5.cloned.1.call-start
  235.3 0.5 all-gather.5.cloned.1.call-update
  235.8 117.0 %all-to-all-done.1 = bf16[16,64,2048]{2,1,0:T(8,128)(2,1)} async-done(((bf16[16,64,2048]{2,1,0:T(8,128)(2,1)}), bf16[16,64,2048]{2,1,0:T(8,128)(2,1)}, u32[]{:S(2)}, u32[]{:S(2)}) %all-to-all-start.1) | async-done | bytes 4194336 | tf_op jit(solution)/shard_map/all_to_all | solution.py:32
  352.8 5.0 %fusion.12 = (f32[1024]{0:T(1024)S(1)}, bf16[1024,2048]{1,0:T(8,128)(2,1)S(1)}) fusion(bf16[16,64,2048]{2,1,0:T(8,128)(2,1)} %all-to-all-done.1, f32[2048]{0:T(1024)S(1)} %copy-done.3, f32[1024]{0:T(1024)S(1)} %add_rsqrt_fusion.1, bf16[1024,2048]{1,0:T(8,128)(2,1)} %param.7), kind=kLoop, calls=%fused_computation.19 | loop fusion | flops 25164800 | bytes 12599296 | tf_op jit(solution)/shard_map/reduce_sum | solution.py:11
  357.8 1.9 copy-done.2
  359.7 3.0 fusion.14
  362.7 14.3 %fusion.28 = f32[4,1024,512]{1,2,0:T(8,128)} fusion(bf16[4,1024,512]{2,1,0:T(8,128)(2,1)} %bitcast.40, bf16[4,512,1024]{2,1,0:T(8,128)(2,1)} %bitcast.39, bf16[128,4,8,512]{3,2,1,0:T(8,128)(2,1)} %bitcast.38), kind=kOutput, calls=%fused_computation.32 | convolution fusion | flops 8627683328 | bytes 20971520 | tf_op jit(solution)/shard_map/rcf,cfd->rcd/dot_general | solution.py:46
  377.1 9.3 %copy.22 = f32[1024,2048]{1,0:T(8,128)} copy(f32[1024,2048]{0,1:T(8,128)} %bitcast.37) | data formatting | bytes 16777216 | tf_op jit(solution)/shard_map/reshape | solution.py:52
  386.4 8.3 %fusion.15 = bf16[1024,2048]{1,0:T(8,128)(2,1)} fusion(f32[1024,2048]{1,0:T(8,128)} %copy.22, bf16[1024,2048]{1,0:T(8,128)(2,1)} %copy-done.2), kind=kLoop, calls=%fused_computation.22 | loop fusion | flops 6291456 | bytes 16777216 | tf_op jit(solution)/shard_map/convert_element_type | solution.py:52
  (15 shorter events, 0.0 us)
Async XLA Ops:
  6.5 3.2 copy-start
  78.3 124.3 %all-to-all-start = ((bf16[16,2,65536]{2,1,0:T(2,128)(2,1)}), bf16[16,2,65536]{2,1,0:T(2,128)(2,1)}, u32[]{:S(2)}, u32[]{:S(2)}) async-start(bf16[16,2,65536]{2,1,0:T(2,128)(2,1)} %reshape.51), calls=%async_computation | async-start | bytes 8388608 | tf_op jit(solution)/shard_map/all_to_all | solution.py:29
  84.8 277.9 %all-gather.3.cloned.1.call-start = ((), (), s32[]{:S(2)}) async-start(), calls=%async_computation.2 | async-start | bytes 4456448 | tf_op jit(solution)/shard_map/all_gather | solution.py:37
  214.9 6.0 %copy-start.5 = (bf16[16,16]{1,0:T(8,128)(2,1)S(1)}, bf16[16,16]{1,0:T(8,128)(2,1)}, u32[]{:S(2)}) copy-start(bf16[16,16]{1,0:T(8,128)(2,1)} %param.11) | copy-start | bytes 1540
  225.8 127.0 %copy-start.3 = (f32[2048]{0:T(1024)S(1)}, f32[2048]{0:T(1024)}, u32[]{:S(2)}) copy-start(f32[2048]{0:T(1024)} %param.8) | copy-start | bytes 24580
  230.1 122.7 %all-to-all-start.1 = ((bf16[16,64,2048]{2,1,0:T(8,128)(2,1)}), bf16[16,64,2048]{2,1,0:T(8,128)(2,1)}, u32[]{:S(2)}, u32[]{:S(2)}) async-start(bf16[16,64,2048]{2,1,0:T(8,128)(2,1)} %copy.19), calls=%async_computation.1 | async-start | bytes 8388608 | tf_op jit(solution)/shard_map/all_to_all | solution.py:32
  235.0 124.7 %copy-start.4 = (f32[2048]{0:T(1024)S(1)}, f32[2048]{0:T(1024)}, u32[]{:S(2)}) copy-start(f32[2048]{0:T(1024)} %param.9) | copy-start | bytes 24580
  235.0 127.7 %all-gather.5.cloned.1.call-start = ((), (), s32[]{:S(2)}) async-start(), calls=%async_computation.3 | async-start | bytes 4456448 | tf_op jit(solution)/shard_map/all_gather | solution.py:45
  357.8 1.9 copy-start.2
  377.1 17.6 %copy-start.1 = (bf16[1024,1024]{1,0:T(8,128)(2,1)S(1)}, bf16[1024,1024]{1,0:T(8,128)(2,1)}, u32[]{:S(2)}) copy-start(bf16[1024,1024]{1,0:T(8,128)(2,1)} %param.10) | copy-start | bytes 6291460
Sparse Core Ops, SparseCore 0:
  87.8 94.8 all-gather.2
  238.0 94.8 all-gather.4
where the time goes:
time: 403 us; the launch traced here: 402 us
  waiting for transfers between devices  235 us (58%)
  local copies, waits for them, and re-layouts  66.5 us (17%)
  other arithmetic  46.3 us (11%)
  matrix products  28.3 us (7%)
  between operations  13.5 us (3%)
  starting transfers between devices  11.9 us (3%)
    all_to_all x1, waiting for transfers between devices, shards(): lax.all_to_all(within, 'seq', split_axis=1, concat_axis=0, tiled=True)  117 us
    all_to_all x1, waiting for transfers between devices, shards(): lax.all_to_all(mixed_cols, 'seq', split_axis=0, concat_axis=1, tiled=True)  117 us
    unnamed x16, local copies, waits for them, and re-layouts  32.2 us
    unnamed x1, other arithmetic  26.7 us
    convert_element_type x1, local copies, waits for them, and re-layouts, shards(): within = jnp.einsum('hp,ops->ohs', block_mix, normed.reshape(nblocks, BLK...  20.6 us
    dot_general x1, matrix products, shards(): jnp.einsum('rcf,cfd->rcd', hidden, weight_out.reshape(NCB, hidden.shape[2...  14.3 us
    reshape x1, local copies, waits for them, and re-layouts, shards(): output.reshape(rows, width)  9.34 us
    dot_general x1, matrix products, shards(): jnp.einsum('hp,ops->ohs', block_mix, normed.reshape(nblocks, BLK, width),...  9.21 us
  transfers between devices with their start and end apart: 4, of which 2 were waited for; matrix products, arithmetic and copies ran while one was open for 9% of the time, Pallas kernels for 0%

commit v1 on v0

--- a/solution.py
+++ b/solution.py
@@ -1,3 +1,4 @@
+import functools
 import jax
 import jax.numpy as jnp
 from jax import lax
@@ -5,6 +6,18 @@
 
 NCB = 4
 BLK = 1024
+
+
+def trails_connect(local_block, device_axis):
+    return jnp.concatenate(
+        lax.all_to_all(
+            jnp.stack(jnp.split(local_block, lax.axis_size(device_axis), axis=1)), device_axis, 0, 0
+        ),
+        axis=0,
+    )
+
+
+measure_desk = functools.partial(trails_connect, device_axis="seq")
 
 
 def rms_scale(values, gain):
@@ -24,10 +37,7 @@
         preferred_element_type=jnp.float32,
     ).astype(jnp.bfloat16)
     mixed_cols = jnp.einsum(
-        "ai,ijd->ajd",
-        cross_mix,
-        lax.all_to_all(within, "seq", split_axis=1, concat_axis=0, tiled=True),
-        preferred_element_type=jnp.float32,
+        "ai,ijd->ajd", cross_mix, measure_desk(within), preferred_element_type=jnp.float32
     ).astype(jnp.bfloat16)
     across = lax.all_to_all(mixed_cols, "seq", split_axis=0, concat_axis=1, tiled=True)
     gated = (

time: 403 us -> 335 us (0.83)
  local copies, waits for them, and re-layouts: 66.5 us -> 27.8 us
  other arithmetic: 46.3 us -> 19.7 us
    unnamed x1 -> x0, other arithmetic: 26.7 us -> none
    convert_element_type x2 -> x1, local copies, waits for them, and re-layouts: 24.9 us -> 4.32 us  [shards(): mixed_cols = jnp.einsum('ai,ijd->ajd', cross_mix, measure_desk(within), p...]
    unnamed x16 -> x29, local copies, waits for them, and re-layouts: 32.2 us -> 13.6 us
    dot_general x1, matrix products: 9.21 us -> 4.96 us  [shards(): jnp.einsum('hp,ops->ohs', block_mix, normed.reshape(nblocks, BLK, width),...]
  transfers between devices with their start and end apart: 4 -> 4, of which waited for: 2 -> 2; matrix products, arithmetic and copies ran while one was open for 9% -> 6% of each run, Pallas kernels for 0% -> 0%
where the time goes in v1:
time: 335 us; the launch traced here: 334 us
  waiting for transfers between devices  235 us (70%)
  local copies, waits for them, and re-layouts  27.8 us (8%)
  matrix products  26.2 us (8%)
  other arithmetic  19.7 us (6%)
  between operations  13.5 us (4%)
  starting transfers between devices  11.9 us (4%)
    all_to_all x1, waiting for transfers between devices, trails_connect(): lax.all_to_all(jnp.stack(jnp.split(local_block, lax.axis_size(device_axis...  117 us
    all_to_all x1, waiting for transfers between devices, shards(): lax.all_to_all(mixed_cols, 'seq', split_axis=0, concat_axis=1, tiled=True)  117 us
    dot_general x1, matrix products, shards(): jnp.einsum('rcf,cfd->rcd', hidden, weight_out.reshape(NCB, hidden.shape[2...  14.3 us
    unnamed x29, local copies, waits for them, and re-layouts  13.6 us
    reshape x1, local copies, waits for them, and re-layouts, shards(): output.reshape(rows, width)  9.2 us
    convert_element_type x1, other arithmetic, shards(): (gated.astype(jnp.float32) + output.reshape(rows, width)).astype(jnp.bflo...  8.44 us
    reduce_sum x2, other arithmetic, rms_scale(): mean_square = jnp.mean(values * values, axis=-1, keepdims=True)  8.22 us
    dot_general x1, matrix products, shards(): jnp.einsum('ai,ijd->ajd', cross_mix, measure_desk(within), preferred_elem...  6.92 us
  transfers between devices with their start and end apart: 4, of which 2 were waited for; matrix products, arithmetic and copies ran while one was open for 6% of the time, Pallas kernels for 0%

profile of v1, /device:TPU:13, one launch (start us, length us, event | category | flops | bytes accessed | tf_op | source)
XLA Modules:
  0.0 334.3 jit_solution(3114427640795503997)
XLA Ops:
  6.5 3.2 fusion.8
  9.8 0.8 copy-done.3
  10.6 5.0 %convert_bitcast_fusion.1 = bf16[1,1024,2048]{2,1,0:T(8,128)(2,1)S(1)} fusion(bf16[1024,1024]{1,0:T(8,128)(2,1)S(1)} %copy-done, bf16[1024,2048]{1,0:T(8,128)(2,1)S(1)} %copy-done.3, f32[2048]{0:T(1024)S(1)} %copy-done.4, f32[1024]{0:T(1024)S(1)} %add_rsqrt_fusion.1), kind=kOutput, calls=%fused_computation.29 | convolution fusion | flops 4305453056 | bytes 10498048 | tf_op jit(solution)/shard_map/hp,ops->ohs/dot_general | solution.py:33
  15.6 0.7 fusion.45
  16.3 0.7 fusion.44
  17.1 0.7 fusion.43
  17.8 0.7 fusion.42
  18.5 0.7 fusion.41
  19.2 0.7 fusion.40
  19.9 0.7 fusion.39
  25.7 0.7 fusion.31
  26.4 0.7 fusion.30
  27.2 6.7 %all-to-all-start = ((bf16[16,1,64,2048]{3,2,1,0:T(8,128)(2,1)}), bf16[16,1,64,2048]{3,2,1,0:T(8,128)(2,1)}, u32[]{:S(2)}, u32[]{:S(2)}) async-start(bf16[16,1,64,2048]{3,2,1,0:T(8,128)(2,1)} %fusion.30), calls=%async_computation | async-start | bytes 8388608 | tf_op jit(solution)/shard_map/all_to_all | solution.py:13
  34.6 117.0 %all-to-all-done = bf16[16,1,64,2048]{3,2,1,0:T(8,128)(2,1)} async-done(((bf16[16,1,64,2048]{3,2,1,0:T(8,128)(2,1)}), bf16[16,1,64,2048]{3,2,1,0:T(8,128)(2,1)}, u32[]{:S(2)}, u32[]{:S(2)}) %all-to-all-start) | async-done | bytes 4194336 | tf_op jit(solution)/shard_map/all_to_all | solution.py:13
  151.6 6.9 %convert_bitcast_fusion = bf16[16,64,2048]{2,0,1:T(8,128)(2,1)S(1)} fusion(bf16[16,64,2048]{2,1,0:T(8,128)(2,1)} %bitcast.19, bf16[16,16]{1,0:T(8,128)(2,1)S(1)} %copy-done.6), kind=kOutput, calls=%fused_computation.28 | convolution fusion | flops 69206016 | bytes 8389120 | tf_op jit(solution)/shard_map/ai,ijd->ajd/dot_general | solution.py:39
  158.5 4.3 %copy.17 = bf16[16,64,2048]{2,1,0:T(8,128)(2,1)} copy(bf16[16,64,2048]{2,0,1:T(8,128)(2,1)S(1)} %convert_bitcast_fusion) | data formatting | bytes 8388608 | tf_op jit(solution)/shard_map/convert_element_type | solution.py:41
  162.8 4.9 %all-to-all-start.1 = ((bf16[16,64,2048]{2,1,0:T(8,128)(2,1)}), bf16[16,64,2048]{2,1,0:T(8,128)(2,1)}, u32[]{:S(2)}, u32[]{:S(2)}) async-start(bf16[16,64,2048]{2,1,0:T(8,128)(2,1)} %copy.17), calls=%async_computation.1 | async-start | bytes 8388608 | tf_op jit(solution)/shard_map/all_to_all | solution.py:42
  168.5 117.0 %all-to-all-done.1 = bf16[16,64,2048]{2,1,0:T(8,128)(2,1)} async-done(((bf16[16,64,2048]{2,1,0:T(8,128)(2,1)}), bf16[16,64,2048]{2,1,0:T(8,128)(2,1)}, u32[]{:S(2)}, u32[]{:S(2)}) %all-to-all-start.1) | async-done | bytes 4194336 | tf_op jit(solution)/shard_map/all_to_all | solution.py:42
  285.5 5.0 %fusion.12 = (f32[1024]{0:T(1024)S(1)}, bf16[1024,2048]{1,0:T(8,128)(2,1)S(1)}) fusion(bf16[16,64,2048]{2,1,0:T(8,128)(2,1)} %all-to-all-done.1, f32[2048]{0:T(1024)S(1)} %copy-done.4, f32[1024]{0:T(1024)S(1)} %add_rsqrt_fusion.1, bf16[1024,2048]{1,0:T(8,128)(2,1)} %param.7), kind=kLoop, calls=%fused_computation.19 | loop fusion | flops 25164800 | bytes 12599296 | tf_op jit(solution)/shard_map/reduce_sum | solution.py:24
  290.5 1.9 copy-done.2
  292.4 3.0 fusion.14
  295.5 14.3 %fusion.28 = f32[4,1024,512]{1,2,0:T(8,128)} fusion(bf16[4,1024,512]{2,1,0:T(8,128)(2,1)} %bitcast.99, bf16[4,512,1024]{2,1,0:T(8,128)(2,1)} %bitcast.98, bf16[128,4,8,512]{3,2,1,0:T(8,128)(2,1)} %bitcast.97), kind=kOutput, calls=%fused_computation.32 | convolution fusion | flops 8627683328 | bytes 20971520 | tf_op jit(solution)/shard_map/rcf,cfd->rcd/dot_general | solution.py:56
  309.8 9.2 %copy.20 = f32[1024,2048]{1,0:T(8,128)} copy(f32[1024,2048]{0,1:T(8,128)} %bitcast.96) | data formatting | bytes 16777216 | tf_op jit(solution)/shard_map/reshape | solution.py:62
  319.0 8.4 %fusion.15 = bf16[1024,2048]{1,0:T(8,128)(2,1)} fusion(f32[1024,2048]{1,0:T(8,128)} %copy.20, bf16[1024,2048]{1,0:T(8,128)(2,1)} %copy-done.2), kind=kLoop, calls=%fused_computation.22 | loop fusion | flops 6291456 | bytes 16777216 | tf_op jit(solution)/shard_map/convert_element_type | solution.py:62
  (27 shorter events, 6.5 us)
Async XLA Ops:
  6.5 3.2 copy-start
  6.5 3.3 copy-start.4
  6.5 4.1 %copy-start.3 = (bf16[1024,2048]{1,0:T(8,128)(2,1)S(1)}, bf16[1024,2048]{1,0:T(8,128)(2,1)}, u32[]{:S(2)}) copy-start(bf16[1024,2048]{1,0:T(8,128)(2,1)} %param.7) | copy-start | bytes 12582916
  27.2 124.4 %copy-start.6 = (bf16[16,16]{1,0:T(8,128)(2,1)S(1)}, bf16[16,16]{1,0:T(8,128)(2,1)}, u32[]{:S(2)}) copy-start(bf16[16,16]{1,0:T(8,128)(2,1)} %param.11) | copy-start | bytes 1540
  27.2 124.4 %all-to-all-start = ((bf16[16,1,64,2048]{3,2,1,0:T(8,128)(2,1)}), bf16[16,1,64,2048]{3,2,1,0:T(8,128)(2,1)}, u32[]{:S(2)}, u32[]{:S(2)}) async-start(bf16[16,1,64,2048]{3,2,1,0:T(8,128)(2,1)} %fusion.30), calls=%async_computation | async-start | bytes 8388608 | tf_op jit(solution)/shard_map/all_to_all | solution.py:13
  33.8 261.6 %all-gather.3.cloned.1.call-start = ((), (), s32[]{:S(2)}) async-start(), calls=%async_computation.2 | async-start | bytes 4456448 | tf_op jit(solution)/shard_map/all_gather | solution.py:47
  162.8 122.7 %all-to-all-start.1 = ((bf16[16,64,2048]{2,1,0:T(8,128)(2,1)}), bf16[16,64,2048]{2,1,0:T(8,128)(2,1)}, u32[]{:S(2)}, u32[]{:S(2)}) async-start(bf16[16,64,2048]{2,1,0:T(8,128)(2,1)} %copy.17), calls=%async_computation.1 | async-start | bytes 8388608 | tf_op jit(solution)/shard_map/all_to_all | solution.py:42
  167.7 127.7 %all-gather.5.cloned.1.call-start = ((), (), s32[]{:S(2)}) async-start(), calls=%async_computation.3 | async-start | bytes 4456448 | tf_op jit(solution)/shard_map/all_gather | solution.py:55
  168.5 124.0 %copy-start.5 = (f32[2048]{0:T(1024)S(1)}, f32[2048]{0:T(1024)}, u32[]{:S(2)}) copy-start(f32[2048]{0:T(1024)} %param.9) | copy-start | bytes 24580
  290.5 1.9 copy-start.2
  319.0 8.4 %copy-start.1 = (bf16[1024,1024]{1,0:T(8,128)(2,1)S(1)}, bf16[1024,1024]{1,0:T(8,128)(2,1)}, u32[]{:S(2)}) copy-start(bf16[1024,1024]{1,0:T(8,128)(2,1)} %param.10) | copy-start | bytes 6291460
Sparse Core Ops, SparseCore 0:
  36.8 94.8 all-gather.2
  170.7 94.8 all-gather.4
